TPU v7x, 768 devices: a whole 4x8x12 slice. The times are simulated.
768 devices in a mesh: loop: 12 (over z_hi, x), outer: 64 (over y, z_lo, core).
Axes of the slice: x: 4, y: 8, z: 12 (z_hi: 3, z_lo: 4; z = z_hi * 4 + z_lo), core: 2. Of those that a mesh axis runs over, the one named last changes fastest.
Arguments:
- note_feats: bfloat16 [196608, 1024], P(('loop', 'outer')), may hold values from -6 to 6
- ehr_feats: bfloat16 [196608, 1024], P(('loop', 'outer')), may hold values from -6 to 6
- note_head: bfloat16 [1024, 1024], replicated, may hold values from -0.1875 to 0.1875
- ehr_head: bfloat16 [1024, 1024], replicated, may hold values from -0.1875 to 0.1875
- logit_scale: float32 [1], replicated, may hold values from 8 to 24
- bias_table: float32 [16], replicated, may hold values from -3 to 0
- bias_index: int32 [196608], P(('loop', 'outer')), may hold values from 0 to 15
Outputs:
- row_loss: float32 [196608], P(('loop', 'outer'))
- note_grad: float32 [196608, 1024], P(('loop', 'outer'))
- ehr_grad: float32 [196608, 1024], P(('loop', 'outer'))
All inputs are finite; a program needn't handle non-finite values.
Results may differ from a plain program's by a relative error of at most 0.0052.
Values may be sent and summed in bfloat16 or wider, within the bound.
A program may use at most 64 MiB of HBM per device.

v0:
```python
import jax
import jax.numpy as jnp
from jax import lax
from jax.sharding import PartitionSpec as P

SHARED = 4


def shifted(x, axis, by):
    devices = lax.axis_size(axis)
    return lax.ppermute(x, axis, [(i, (i + by) % devices) for i in range(devices)])


def unit_rows(features, head_matrix):
    projected = jnp.dot(features, head_matrix, preferred_element_type=jnp.float32)
    inverse = lax.rsqrt(jnp.sum(projected * projected, axis=-1, keepdims=True) + 1e-06)
    return (projected * inverse, inverse)


def unit_back(normed, inverse, upstream, head_matrix):
    radial = jnp.sum(normed * upstream, axis=-1, keepdims=True)
    pre_grad = (inverse * (upstream - normed * radial)).astype(jnp.bfloat16)
    return lax.dot_general(
        pre_grad, head_matrix, (((1,), (1,)), ((), ())), preferred_element_type=jnp.float32
    )


def per_device(note_feats, ehr_feats, note_head, ehr_head, logit_scale, bias_table, bias_index):
    note_unit, note_inverse = unit_rows(note_feats, note_head)
    ehr_unit, ehr_inverse = unit_rows(ehr_feats, ehr_head)
    note_emb = note_unit.astype(jnp.bfloat16)
    record_emb = ehr_unit.astype(jnp.bfloat16)
    own_shared = note_emb[:SHARED]
    side_pieces = [shifted(own_shared, "loop", offset) for offset in (1, -1)]
    below_set, above_set = (
        lax.all_gather(side_pieces[0], "outer", axis=0, tiled=True),
        lax.all_gather(side_pieces[1], "outer", axis=0, tiled=True),
    )
    window = jnp.concatenate([note_emb, below_set, above_set], axis=0)
    bundle_rows = below_set.shape[0]
    pairs_here = note_emb.shape[0]
    multiplier = logit_scale[0]
    classes = lax.broadcasted_iota(jnp.int32, (pairs_here, bias_table.shape[0]), 1)
    offsets = jnp.sum(
        jnp.where(bias_index[:, None] == classes, bias_table[None, :], 0.0), axis=1, keepdims=True
    )
    similar = lax.dot_general(
        record_emb, window, (((1,), (1,)), ((), ())), preferred_element_type=jnp.float32
    )
    logits = multiplier * similar + offsets
    columns = lax.broadcasted_iota(jnp.int32, logits.shape, 1)
    row_ids = lax.broadcasted_iota(jnp.int32, logits.shape, 0)
    labels = jnp.where(columns == row_ids, 1.0, -1.0).astype(jnp.float32)
    margins = -labels * logits
    row_loss = jnp.mean(jax.nn.softplus(margins), axis=-1)
    slopes = (-labels * jax.nn.sigmoid(margins)).astype(jnp.bfloat16)
    record_upstream = multiplier * jnp.dot(slopes, window, preferred_element_type=jnp.float32)
    window_grad = multiplier * lax.dot_general(
        slopes, record_emb, (((0,), (0,)), ((), ())), preferred_element_type=jnp.float32
    )
    local_part = window_grad[:pairs_here]
    below_part = window_grad[pairs_here : pairs_here + bundle_rows]
    above_part = window_grad[pairs_here + bundle_rows :]
    blocks = jnp.stack([below_part, above_part], axis=0)
    shares = lax.psum_scatter(blocks, "outer", scatter_dimension=1, tiled=True)
    returned = [shifted(shares[position], "loop", offset) for position, offset in ((0, -1), (1, 1))]
    shared_up = returned[0] + returned[1]
    note_upstream = jnp.concatenate([local_part[:SHARED] + shared_up, local_part[SHARED:]], axis=0)
    note_grad = unit_back(note_unit, note_inverse, note_upstream, note_head)
    ehr_grad = unit_back(ehr_unit, ehr_inverse, record_upstream, ehr_head)
    return (row_loss, note_grad, ehr_grad)


def solution(mesh):
    return jax.shard_map(
        per_device,
        mesh=mesh,
        in_specs=(
            P(("loop", "outer"), None),
            P(("loop", "outer"), None),
            P(),
            P(),
            P(),
            P(),
            P(("loop", "outer")),
        ),
        out_specs=(P(("loop", "outer")), P(("loop", "outer"), None), P(("loop", "outer"), None)),
        check_vma=False,
    )
```

profile of v0, /device:TPU:32, one launch (start us, length us, event | category | flops | bytes accessed | tf_op | source)
XLA Modules:
  0.0 788.4 jit_solution(8485761047191347616)
XLA Ops:
  7.2 0.0 all-reduce.3.cloned.1.call-start
  7.2 2.7 multiply_reduce_fusion.2
  9.9 0.1 multiply_convert_fusion.2
  10.1 0.8 copy-done.5
  10.9 3.5 collective-permute-start
  14.4 15.3 %collective-permute-start.1 = (bf16[4,1024]{1,0:T(4,128)(2,1)S(1)}, bf16[4,1024]{1,0:T(4,128)(2,1)S(1)}, u32[]{:S(2)}, u32[]{:S(2)}) collective-permute-start(bf16[4,1024]{1,0:T(4,128)(2,1)S(1)} %slice.31), channel_id=1, source_target_pairs={{0,704},{64,0},{128,64},{192,128},{256,192},{320,256},{384,320},{4... | collective-permute-start | bytes 24584 | tf_op jit(solution)/shard_map/ppermute | solution.py:11
  29.7 1.7 multiply_reduce_fusion.3
  31.4 0.1 select_reduce_fusion
  32.2 84.1 %all-gather = bf16[64,4,1024]{2,1,0:T(4,128)(2,1)} all-gather(bf16[1,4,1024]{2,1,0:T(4,128)(2,1)S(1)} %bitcast.24), channel_id=1, replica_groups=mesh['loop'=12,'outer'=64] {'outer'}, dimensions={0}, use_global_device_ids=true | all-gather | bytes 532480 | tf_op jit(solution)/shard_map/all_gather | solution.py:36
  116.3 2.0 reshape.24
  118.3 81.2 %all-gather.1 = bf16[64,4,1024]{2,1,0:T(4,128)(2,1)} all-gather(bf16[1,4,1024]{2,1,0:T(4,128)(2,1)S(1)} %bitcast.23), channel_id=1, replica_groups=mesh['loop'=12,'outer'=64] {'outer'}, dimensions={0}, use_global_device_ids=true | all-gather | bytes 532480 | tf_op jit(solution)/shard_map/all_gather | solution.py:37
  199.5 2.0 reshape.26
  201.5 2.7 fusion.2
  204.2 0.9 copy-done.9
  205.1 0.7 convolution_multiply_fusion
  205.8 0.2 slice_bitcast_fusion.1
  206.1 1.4 copy-done.4
  207.5 1.5 pad_maximum_fusion
  209.0 0.0 all-reduce.3.cloned.1.call-update
  209.0 1.3 dynamic-slice
  211.0 2.7 multiply_reduce_fusion
  213.7 1.8 fusion.4
  215.5 539.9 %all-reduce.3.cloned.1.call-done = f32[2,256,1024]{2,1,0:T(8,128)} async-done(((f32[2,256,1024]{2,1,0:T(8,128)}), f32[2,256,1024]{2,1,0:T(8,128)}) %all-reduce.3.cloned.1.call-update) | async-done | bytes 2097168
  755.4 0.8 dynamic-slice_bitcast_fusion
  756.2 10.8 %collective-permute-start.2 = (f32[4,1024]{1,0:T(4,128)S(1)}, f32[4,1024]{1,0:T(4,128)S(1)}, u32[]{:S(2)}, u32[]{:S(2)}) collective-permute-start(f32[4,1024]{1,0:T(4,128)S(1)} %get-tuple-element.6), channel_id=1, source_target_pairs={{0,704},{64,0},{128,64},{192,128},{256,192},{320,256},{384,320},{4... | collective-permute-start | bytes 49160 | tf_op jit(solution)/shard_map/ppermute | solution.py:11
  767.0 1.9 collective-permute-start.3
  768.9 0.6 broadcast_multiply_fusion
  769.5 1.5 slice.35
  771.0 7.7 collective-permute-done.3
  778.7 0.8 slice_add_fusion
  779.4 0.3 multiply_reduce_fusion.1
  779.8 1.8 fusion.3
  (23 shorter events, 0.1 us)
Async XLA Ops:
  7.2 22.5 %copy-start = (bf16[1024,1024]{1,0:T(8,128)(2,1)S(1)}, bf16[1024,1024]{1,0:T(8,128)(2,1)}, u32[]{:S(2)}) copy-start(bf16[1024,1024]{1,0:T(8,128)(2,1)} %param.10) | copy-start | bytes 6291460
  7.2 748.2 %all-reduce.3.cloned.1.call-start = ((), (), s32[]{:S(2)}) async-start(), calls=%async_computation | async-start | bytes 4194304
  7.2 22.5 %copy-start.6 = (bf16[256,1024]{1,0:T(8,128)(2,1)S(1)}, bf16[256,1024]{1,0:T(8,128)(2,1)}, u32[]{:S(2)}) copy-start(bf16[256,1024]{1,0:T(8,128)(2,1)} %param.8) | copy-start | bytes 1572868
  10.1 0.8 copy-start.5
  10.9 20.5 %copy-start.7 = (s32[256]{0:T(256)S(1)}, s32[256]{0:T(256)}, u32[]{:S(2)}) copy-start(s32[256]{0:T(256)} %param.13) | copy-start | bytes 3076
  10.9 20.5 %copy-start.8 = (f32[16]{0:T(128)S(1)}, f32[16]{0:T(128)}, u32[]{:S(2)}) copy-start(f32[16]{0:T(128)} %param.12) | copy-start | bytes 196
  10.9 21.3 %collective-permute-start = (bf16[4,1024]{1,0:T(4,128)(2,1)S(1)}, bf16[4,1024]{1,0:T(4,128)(2,1)S(1)}, u32[]{:S(2)}, u32[]{:S(2)}) collective-permute-start(bf16[4,1024]{1,0:T(4,128)(2,1)S(1)} %slice.31), channel_id=1, source_target_pairs={{0,64},{64,128},{128,192},{192,256},{256,320},{320,384},{384,448},... | collective-permute-start | bytes 24584 | tf_op jit(solution)/shard_map/ppermute | solution.py:11
  14.4 103.8 %collective-permute-start.1 = (bf16[4,1024]{1,0:T(4,128)(2,1)S(1)}, bf16[4,1024]{1,0:T(4,128)(2,1)S(1)}, u32[]{:S(2)}, u32[]{:S(2)}) collective-permute-start(bf16[4,1024]{1,0:T(4,128)(2,1)S(1)} %slice.31), channel_id=1, source_target_pairs={{0,704},{64,0},{128,64},{192,128},{256,192},{320,256},{384,320},{4... | collective-permute-start | bytes 24584 | tf_op jit(solution)/shard_map/ppermute | solution.py:11
  201.5 3.6 copy-start.2
  204.2 0.9 copy-start.9
  205.8 1.7 copy-start.4
  210.9 2.8 copy-start.3
  756.2 14.8 %collective-permute-start.2 = (f32[4,1024]{1,0:T(4,128)S(1)}, f32[4,1024]{1,0:T(4,128)S(1)}, u32[]{:S(2)}, u32[]{:S(2)}) collective-permute-start(f32[4,1024]{1,0:T(4,128)S(1)} %get-tuple-element.6), channel_id=1, source_target_pairs={{0,704},{64,0},{128,64},{192,128},{256,192},{320,256},{384,320},{4... | collective-permute-start | bytes 49160 | tf_op jit(solution)/shard_map/ppermute | solution.py:11
  767.0 11.6 %collective-permute-start.3 = (f32[4,1024]{1,0:T(4,128)S(1)}, f32[4,1024]{1,0:T(4,128)S(1)}, u32[]{:S(2)}, u32[]{:S(2)}) collective-permute-start(f32[4,1024]{1,0:T(4,128)S(1)} %get-tuple-element.5), channel_id=1, source_target_pairs={{0,64},{64,128},{128,192},{192,256},{256,320},{320,384},{384,448},... | collective-permute-start | bytes 49160 | tf_op jit(solution)/shard_map/ppermute | solution.py:11
  769.5 10.2 %copy-start.1 = (bf16[1024,1024]{1,0:T(8,128)(2,1)S(1)}, bf16[1024,1024]{1,0:T(8,128)(2,1)}, u32[]{:S(2)}) copy-start(bf16[1024,1024]{1,0:T(8,128)(2,1)} %param.9) | copy-start | bytes 6291460
Sparse Core Ops, SparseCore 0:
  209.1 546.2 all-reduce.2
where the time goes:
time: 789 us; the launch traced here: 788 us
  waiting for transfers between devices  548 us (69%)
  blocking collectives  165 us (21%)
  starting transfers between devices  31.6 us (4%)
  between operations  15.5 us (2%)
  matrix products  14.2 us (2%)
  local copies, waits for them, and re-layouts  10.9 us (1%)
    unnamed x2, waiting for transfers between devices  540 us
    all_gather x1, blocking collectives, per_device(): lax.all_gather(side_pieces[0], 'outer', axis=0, tiled=True)  84.1 us
    all_gather x1, blocking collectives, per_device(): lax.all_gather(side_pieces[1], 'outer', axis=0, tiled=True)  81.2 us
    ppermute x4, starting transfers between devices, shifted(): lax.ppermute(x, axis, [(i, (i + by) % devices) for i in range(devices)])  31.5 us
  transfers between devices with their start and end apart: 5, of which 2 were waited for; matrix products, arithmetic and copies ran while one was open for 1% of the time, Pallas kernels for 0%

commit v1 on v0

v1 whole, which is shorter than its diff:
```python
import functools

import jax
import jax.numpy as jnp
from jax import lax
from jax.experimental import pallas as pl
from jax.experimental.pallas import tpu as pltpu
from jax.sharding import PartitionSpec as P

SHARED = 4
Z = 4
CORES = 2
BLOCK = SHARED * Z
MESH = pl.DeviceIdType.MESH
NT = (((1,), (1,)), ((), ()))
TN = (((0,), (0,)), ((), ()))


def dot(a, b, dims=(((1,), (0,)), ((), ()))):
    return lax.dot_general(a, b, dims, preferred_element_type=jnp.float32)


def terms(margins):
    t = jnp.exp(-jnp.abs(margins))
    r = 1.0 / (1.0 + t)
    return jnp.maximum(margins, 0.0) + jnp.log1p(t), jnp.where(margins >= 0.0, r, t * r)


def upper_half(shape):
    return lax.broadcasted_iota(jnp.int32, shape, 0) < SHARED


def pack(rows):
    w = rows.shape[1] // 4
    c = [rows[:, q * w : (q + 1) * w] for q in range(4)]
    up = upper_half(c[0].shape)
    lo = jnp.where(up, c[0], pltpu.roll(c[1], SHARED, 0))
    hi = jnp.where(up, c[2], pltpu.roll(c[3], SHARED, 0))
    return jnp.concatenate([lo, hi], axis=0)


def unpack_pair(first, second):
    up = upper_half((8, first.shape[1]))
    out = []
    for half in range(2):
        a, b = first[half * 8 : half * 8 + 8], second[half * 8 : half * 8 + 8]
        out.append(jnp.where(up, a, pltpu.roll(b, SHARED, 0)))
        out.append(jnp.where(up, pltpu.roll(a, SHARED, 0), b))
    return jnp.concatenate(out, axis=1)


def kernel(
    n_loop, ring,
    nf_hbm, ef_hbm, nh_hbm, eh_hbm, scale_ref, table_ref, index_ref,
    loss_ref, ng_hbm, eg_hbm,
    nf, ef, nh, eh, nu, ru, ninv, rinv, ne, re, off, off_out,
    pieces, own_piece, W, G, S, R, back_out, back, slopes, local_slopes,
    lossacc, loss_out, loss_in, rup, rup_out, rup_in, nup, pre, out_n, out_e, tail,
    load_sem, store_sem, piece_send, piece_recv, ag_send, ag_recv, rs_send, rs_recv,
    back_send, back_recv, sib_send, sib_recv,
):
    pairs, width = nf.shape
    far = ring // 2
    tile = min(256, width)
    tiles = width // tile
    l, o = lax.axis_index("loop"), lax.axis_index("outer")
    c, z, y = lax.rem(o, CORES), lax.rem(o // CORES, Z), o // (CORES * Z)

    def outer(yy, zz, cc):
        return (yy * Z + zz) * CORES + cc

    below, above = lax.rem(l + n_loop - 1, n_loop), lax.rem(l + 1, n_loop)
    ahead = (l, outer(lax.rem(y + 1, ring), z, c))
    behind = (l, outer(lax.rem(y + ring - 1, ring), z, c))
    sibling = (l, outer(y, z, 1 - c))
    zs = [lax.rem(z + d, Z) for d in range(Z)]

    barrier = pltpu.get_barrier_semaphore()
    partners = [ahead, behind, sibling]
    partners += [(p, outer(y, zz, c)) for p in (below, above) for zz in zs]
    for partner in partners:
        pl.semaphore_signal(barrier, inc=1, device_id=partner, device_id_type=MESH)

    loads = [
        pltpu.make_async_copy(src, dst, load_sem.at[i])
        for i, (src, dst) in enumerate(((nh_hbm, nh), (nf_hbm, nf), (eh_hbm, eh), (ef_hbm, ef)))
    ]
    for load in loads:
        load.start()

    def remote(src, dst, send, recv, device):
        return pltpu.make_async_remote_copy(
            src_ref=src, dst_ref=dst, send_sem=send, recv_sem=recv, device_id=device, device_id_type=MESH
        )

    def project(feats, head, unit):
        def step(j, carry):
            cols = pl.ds(pl.multiple_of(j * tile, tile), tile)
            unit[:, cols] = dot(feats[...], head[:, cols])
            return carry

        lax.fori_loop(0, tiles, step, 0)

    def normalise(unit, inverse, emb):
        step_rows = min(64, pairs)

        def step(j, carry):
            rows = pl.ds(pl.multiple_of(j * step_rows, step_rows), step_rows)
            p = unit[rows, :]
            inv = lax.rsqrt(jnp.sum(p * p, axis=-1, keepdims=True) + 1e-06)
            u = p * inv
            inverse[rows, :] = inv
            unit[rows, :] = u
            emb[rows, :] = u.astype(jnp.bfloat16)
            return carry

        lax.fori_loop(0, pairs // step_rows, step, 0)

    loads[0].wait()
    loads[1].wait()
    project(nf, nh, nu)
    top = nu[0:8, :]
    top = top * lax.rsqrt(jnp.sum(top * top, axis=-1, keepdims=True) + 1e-06)
    own_piece[...] = pack(top).astype(jnp.bfloat16)
    pl.semaphore_wait(barrier, len(partners))
    piece_copies = []
    for side, pod in ((0, above), (1, below)):
        for d in range(Z):
            k = side * Z + d
            piece_copies.append(
                remote(own_piece, pieces.at[k], piece_send.at[k], piece_recv.at[k], (pod, outer(y, zs[d], c)))
            )
            piece_copies[-1].start()
    normalise(nu, ninv, ne)

    loads[2].wait()
    loads[3].wait()
    project(ef, eh, ru)
    normalise(ru, rinv, re.at[pl.ds(0, pairs)])
    index = index_ref[...]
    offsets = jnp.zeros(index.shape, jnp.float32)
    for k in range(table_ref.shape[0]):
        offsets = jnp.where(index == k, table_ref[k], offsets)
    off_out[...] = jnp.broadcast_to(offsets, off_out.shape)
    sib_rec = remote(re.at[pl.ds(0, pairs)], re.at[pl.ds(pairs, pairs)], sib_send.at[0], sib_recv.at[0], sibling)
    sib_off = remote(off_out, off, sib_send.at[1], sib_recv.at[1], sibling)
    sib_rec.start()
    sib_off.start()

    def reach(side, way):
        return far if (side == 0) == (way == 1) else far - 1

    def slot(side, way, dist):
        if dist == 0:
            return side
        if dist == far:
            return 2 + 4 * (far - 1) + side
        return 2 + 4 * (dist - 1) + 2 * (way < 0) + side

    def rows_of(s):
        return pl.ds(s * BLOCK, BLOCK)

    scale = scale_ref[0]
    for copy in piece_copies:
        copy.wait_recv()
    for side in range(2):
        p = [pieces[side * Z + d].astype(jnp.float32) for d in range(Z)]
        block = jnp.concatenate([unpack_pair(p[0], p[1]), unpack_pair(p[2], p[3])], axis=0)
        W[side * BLOCK : (side + 1) * BLOCK, :] = block.astype(jnp.bfloat16)

    gathers = {}

    def forward(side, way, dist):
        src, dst = slot(side, way, dist), slot(side, way, dist + 1)
        copy = remote(
            W.at[rows_of(src)], W.at[rows_of(dst)], ag_send.at[dst - 2], ag_recv.at[dst - 2],
            ahead if way == 1 else behind,
        )
        copy.start()
        gathers[side, way, dist + 1] = copy

    chains = [(0, 1), (1, -1), (1, 1), (0, -1)]
    for side, way in chains:
        forward(side, way, 0)

    sims = dot(ne[...], re[0:pairs, :], NT)
    logits = scale * sims + offsets
    positive = lax.broadcasted_iota(jnp.int32, logits.shape, 0) == lax.broadcasted_iota(jnp.int32, logits.shape, 1)
    softplus, sigmoid = terms(jnp.where(positive, -logits, logits))
    local_slopes[...] = jnp.where(positive, -sigmoid, sigmoid).astype(jnp.bfloat16)
    lossacc[:, 0:pairs] = jnp.sum(softplus.reshape(pairs // 8, 8, pairs), axis=0)
    lossacc[:, pairs:] = jnp.zeros((8, pairs), jnp.float32)

    sib_off.wait_recv()
    sib_rec.wait_recv()
    all_offsets = jnp.concatenate([off_out[0:1, :], off[0:1, :]], axis=1)

    def notes(first, count):
        rows = slice(first * BLOCK, (first + count) * BLOCK)
        n = count * BLOCK
        logits = scale * dot(W[rows, :], re[...], NT) + all_offsets
        softplus, sigmoid = terms(logits)
        lossacc[...] += jnp.sum(softplus.reshape(n // 8, 8, 2 * pairs), axis=0)
        s = sigmoid.astype(jnp.bfloat16)
        slopes[rows, :] = s
        G[rows, :] = dot(s, re[...])

    reduces = {}

    def reduce_from(side, way, dist):
        s = slot(side, way, dist)
        rows = slice(s * BLOCK, (s + 1) * BLOCK)
        total = G[rows, :]
        if dist < reach(side, way):
            reduces[side, way, dist + 1].wait_recv()
            total = total + R[slot(side, way, dist + 1) - 2].astype(jnp.float32)
        S[s - 2] = total.astype(jnp.bfloat16)
        copy = remote(
            S.at[s - 2], R.at[s - 2], rs_send.at[s - 2], rs_recv.at[s - 2], behind if way == 1 else ahead
        )
        copy.start()
        reduces[side, way, dist] = copy

    notes(0, 2)
    for dist in range(1, far):
        for side, way in chains:
            gathers[side, way, dist].wait_recv()
            if dist < reach(side, way):
                forward(side, way, dist)
        notes(2 + 4 * (dist - 1), 4)
    short = [(1, 1), (0, -1)]
    long = [(0, 1), (1, -1)]
    if far > 1:
        for side, way in short:
            reduce_from(side, way, far - 1)
    for side, way in long:
        gathers[side, way, far].wait_recv()
    notes(2 + 4 * (far - 1), 2)
    for side, way in long:
        reduce_from(side, way, far)

    def upstream_sibling(j, carry):
        cols = pl.ds(pl.multiple_of(j * tile, tile), tile)
        rup_out[:, cols] = dot(slopes[:, pairs:], W[:, cols], TN)
        return carry

    def upstream_own(j, carry):
        cols = pl.ds(pl.multiple_of(j * tile, tile), tile)
        rup[:, cols] = dot(slopes[:, 0:pairs], W[:, cols], TN) + dot(local_slopes[...], ne[:, cols], TN)
        return carry

    def upstream_notes(j, carry):
        cols = pl.ds(pl.multiple_of(j * tile, tile), tile)
        nup[:, cols] = scale * dot(local_slopes[...], re[0:pairs, cols])
        return carry

    def back_grad(head, out):
        def step(j, carry):
            cols = pl.ds(pl.multiple_of(j * tile, tile), tile)
            out[:, cols] = dot(pre[...], head[cols, :], NT)
            return carry

        lax.fori_loop(0, tiles, step, 0)

    def pre_grads(unit, inverse, upstream):
        step_rows = min(64, pairs)

        def step(j, carry):
            rows = pl.ds(pl.multiple_of(j * step_rows, step_rows), step_rows)
            u, up = unit[rows, :], upstream(rows)
            radial = jnp.sum(u * up, axis=-1, keepdims=True)
            pre[rows, :] = (inverse[rows, :] * (up - u * radial)).astype(jnp.bfloat16)
            return carry

        lax.fori_loop(0, pairs // step_rows, step, 0)

    def reduce_step(dist):
        if 1 <= dist - 1:
            for side, way in short:
                reduce_from(side, way, dist - 1)
        if 1 <= dist:
            for side, way in long:
                reduce_from(side, way, dist)

    lax.fori_loop(0, tiles, upstream_sibling, 0)
    loss_out[...] = lossacc[:, pairs:]
    sib_rup = remote(rup_out, rup_in, sib_send.at[2], sib_recv.at[2], sibling)
    sib_loss = remote(loss_out, loss_in, sib_send.at[3], sib_recv.at[3], sibling)
    sib_rup.start()
    sib_loss.start()
    stores = []

    def filler_a():
        lax.fori_loop(0, tiles, upstream_own, 0)

    def filler_b():
        lax.fori_loop(0, tiles, upstream_notes, 0)
        pre_grads(nu, ninv, lambda rows: nup[rows, :])
        back_grad(nh, out_n)
        copy = pltpu.make_async_copy(
            out_n.at[pl.ds(8, pairs - 8)], ng_hbm.at[pl.ds(8, pairs - 8)], store_sem.at[0]
        )
        copy.start()
        stores.append(copy)

    def filler_c():
        sib_rup.wait_recv()
        sib_loss.wait_recv()
        loss = jnp.sum(lossacc[:, 0:pairs] + loss_in[...], axis=0, keepdims=True)
        loss_ref[...] = loss * (1.0 / (pairs + ring * Z * CORES * SHARED * 2))
        pre_grads(ru, rinv, lambda rows: scale * (rup[rows, :] + rup_in[rows, :]))
        back_grad(eh, out_e)
        copy = pltpu.make_async_copy(out_e, eg_hbm, store_sem.at[1])
        copy.start()
        stores.append(copy)

    fillers = [filler_a, filler_b, filler_c]
    for dist in range(far - 1, 0, -1):
        reduce_step(dist)
        if fillers:
            fillers.pop(0)()
    for filler in fillers:
        filler()

    returns = []
    for side in range(2):
        total = G[side * BLOCK : (side + 1) * BLOCK, :]
        for way in (1, -1):
            if reach(side, way) > 0:
                reduces[side, way, 1].wait_recv()
                total = total + R[slot(side, way, 1) - 2].astype(jnp.float32)
        total = scale * total
        for d in range(Z):
            half = total[(d // 2) * 8 : (d // 2) * 8 + 8, :]
            if d % 2:
                half = pltpu.roll(half, SHARED, 0)
            k = side * Z + d
            back_out[k] = pack(half).astype(jnp.bfloat16)
            owner_z = lax.rem(z + Z - d, Z)
            copy = remote(
                back_out.at[k], back.at[k], back_send.at[k], back_recv.at[k],
                (below if side == 0 else above, outer(y, owner_z, c)),
            )
            copy.start()
            returns.append(copy)

    total = None
    for k, copy in enumerate(returns):
        copy.wait_recv()
        part = back[k].astype(jnp.float32)
        total = part if total is None else total + part
    lo, hi = total[0:8], total[8:16]
    spread = jnp.concatenate([lo, pltpu.roll(lo, SHARED, 0), hi, pltpu.roll(hi, SHARED, 0)], axis=1)
    up = nup[0:8, :] + jnp.where(upper_half(spread.shape), spread, 0.0)
    u = nu[0:8, :]
    radial = jnp.sum(u * up, axis=-1, keepdims=True)
    g = (ninv[0:8, :] * (up - u * radial)).astype(jnp.bfloat16)
    tail[...] = dot(g, nh[...], NT)
    last = pltpu.make_async_copy(tail, ng_hbm.at[pl.ds(0, 8)], store_sem.at[2])
    last.start()
    stores.append(last)

    sent = piece_copies + list(gathers.values()) + list(reduces.values()) + returns
    for copy in sent + [sib_rec, sib_off, sib_rup, sib_loss]:
        copy.wait_send()
    for copy in stores:
        copy.wait()


def per_device(n_loop, n_outer, note_feats, ehr_feats, note_head, ehr_head, logit_scale, bias_table, bias_index):
    pairs, width = note_feats.shape
    emb = note_head.shape[1]
    ring = n_outer // (Z * CORES)
    blocks = 2 * ring
    held = blocks * BLOCK
    bf16, f32 = jnp.bfloat16, jnp.float32
    vmem = pltpu.VMEM
    dma = pltpu.SemaphoreType.DMA
    hbm = pl.BlockSpec(memory_space=pl.ANY)
    smem = pl.BlockSpec(memory_space=pltpu.SMEM)
    whole = pl.BlockSpec(memory_space=pltpu.VMEM)
    loss, note_grad, ehr_grad = pl.pallas_call(
        functools.partial(kernel, n_loop, ring),
        out_shape=(
            jax.ShapeDtypeStruct((1, pairs), f32),
            jax.ShapeDtypeStruct((pairs, width), f32),
            jax.ShapeDtypeStruct((pairs, width), f32),
        ),
        in_specs=[hbm] * 4 + [smem, smem, whole],
        out_specs=(whole, hbm, hbm),
        scratch_shapes=[
            vmem((pairs, width), bf16),
            vmem((pairs, width), bf16),
            vmem((width, emb), bf16),
            vmem((width, emb), bf16),
            vmem((pairs, emb), f32),
            vmem((pairs, emb), f32),
            vmem((pairs, 1), f32),
            vmem((pairs, 1), f32),
            vmem((pairs, emb), bf16),
            vmem((2 * pairs, emb), bf16),
            vmem((8, pairs), f32),
            vmem((8, pairs), f32),
            vmem((2 * Z, BLOCK, emb // 4), bf16),
            vmem((BLOCK, emb // 4), bf16),
            vmem((held, emb), bf16),
            vmem((held, emb), f32),
            vmem((blocks - 2, BLOCK, emb), bf16),
            vmem((blocks - 2, BLOCK, emb), bf16),
            vmem((2 * Z, BLOCK, emb // 4), bf16),
            vmem((2 * Z, BLOCK, emb // 4), bf16),
            vmem((held, 2 * pairs), bf16),
            vmem((pairs, pairs), bf16),
            vmem((8, 2 * pairs), f32),
            vmem((8, pairs), f32),
            vmem((8, pairs), f32),
            vmem((pairs, emb), f32),
            vmem((pairs, emb), f32),
            vmem((pairs, emb), f32),
            vmem((pairs, emb), f32),
            vmem((pairs, emb), bf16),
            vmem((pairs, width), f32),
            vmem((pairs, width), f32),
            vmem((8, width), f32),
            dma((4,)),
            dma((3,)),
            dma((2 * Z,)),
            dma((2 * Z,)),
            dma((blocks - 2,)),
            dma((blocks - 2,)),
            dma((blocks - 2,)),
            dma((blocks - 2,)),
            dma((2 * Z,)),
            dma((2 * Z,)),
            dma((4,)),
            dma((4,)),
        ],
        compiler_params=pltpu.CompilerParams(
            collective_id=0, has_side_effects=True, vmem_limit_bytes=48 * 1024 * 1024
        ),
    )(note_feats, ehr_feats, note_head, ehr_head, logit_scale, bias_table, bias_index.reshape(1, pairs))
    return loss.reshape(pairs), note_grad, ehr_grad


def solution(mesh):
    return jax.shard_map(
        functools.partial(per_device, mesh.shape["loop"], mesh.shape["outer"]),
        mesh=mesh,
        in_specs=(
            P(("loop", "outer"), None),
            P(("loop", "outer"), None),
            P(),
            P(),
            P(),
            P(),
            P(("loop", "outer")),
        ),
        out_specs=(P(("loop", "outer")), P(("loop", "outer"), None), P(("loop", "outer"), None)),
        check_vma=False,
    )
```

time: 789 us -> 70.4 us (0.09)
  the two profiles are of different devices: /device:TPU:32 before, /device:TPU:8 now
where the time goes in v1:
time: 70.4 us; the launch traced here: 70.1 us
  Pallas kernels  61.3 us (87%)
  local copies, waits for them, and re-layouts  7.5 us (11%)
  between operations  1.3 us (2%)
    pallas_call x1, Pallas kernels, per_device(): pl.pallas_call(functools.partial(kernel, n_loop, ring), out_shape=(jax.Sh...  61.3 us
    unnamed x13, local copies, waits for them, and re-layouts  7.5 us

profile of v1, /device:TPU:8, one launch (start us, length us, event | category | flops | bytes accessed | tf_op | source)
XLA Modules:
  0.0 70.1 jit_solution(2658806747352261238)
XLA Ops:
  1.3 0.0 copy-start
  1.3 1.6 %copy-done = bf16[1024,1024]{1,0:T(8,128)(2,1)S(1)} copy-done((bf16[1024,1024]{1,0:T(8,128)(2,1)S(1)}, bf16[1024,1024]{1,0:T(8,128)(2,1)}, u32[]{:S(2)}) %copy-start) | copy-done | bytes 2097176
  2.9 0.0 copy-start.1
  2.9 1.0 %copy-done.1 = bf16[256,1024]{1,0:T(8,128)(2,1)S(1)} copy-done((bf16[256,1024]{1,0:T(8,128)(2,1)S(1)}, bf16[256,1024]{1,0:T(8,128)(2,1)}, u32[]{:S(2)}) %copy-start.1) | copy-done | bytes 524312
  3.9 0.0 copy-start.2
  3.9 1.0 %copy-done.2 = bf16[256,1024]{1,0:T(8,128)(2,1)S(1)} copy-done((bf16[256,1024]{1,0:T(8,128)(2,1)S(1)}, bf16[256,1024]{1,0:T(8,128)(2,1)}, u32[]{:S(2)}) %copy-start.2) | copy-done | bytes 524312
  5.0 0.0 copy-start.3
  5.0 0.7 copy-done.3
  5.6 0.0 copy-start.4
  5.6 0.7 copy-done.4
  6.3 61.3 %shard_map.94 = (f32[1,256]{1,0:T(1,128)S(1)}, f32[256,1024]{1,0:T(8,128)S(1)}, f32[256,1024]{1,0:T(8,128)S(1)}) custom-call(bf16[256,1024]{1,0:T(8,128)(2,1)S(1)} %copy-done.1, bf16[256,1024]{1,0:T(8,128)(2,1)S(1)} %copy-done.2, bf16[1024,1024]{1,0:T(8,128)(2,1)S(1)} %copy-done, bf16[1024,1024]{1,0:T(8,128)(2,1)} %eh_hbm.1, f32[1]{0:T(128)S(6)} %copy.13.scale_ref, ...), custom_call_target="tpu_custom_call" | custom-call | tf_op jit(solution)/shard_map/pallas_call | solution.py:382
  67.6 0.6 copy.14
  68.1 1.0 %copy.15 = f32[256,1024]{1,0:T(8,128)} copy(f32[256,1024]{1,0:T(8,128)S(1)} %get-tuple-element.13) | data formatting | bytes 2097152
  69.1 1.0 %copy.16 = f32[256,1024]{1,0:T(8,128)} copy(f32[256,1024]{1,0:T(8,128)S(1)} %get-tuple-element.14) | data formatting | bytes 2097152
Async XLA Ops:
  1.3 1.6 %copy-start = (bf16[1024,1024]{1,0:T(8,128)(2,1)S(1)}, bf16[1024,1024]{1,0:T(8,128)(2,1)}, u32[]{:S(2)}) copy-start(bf16[1024,1024]{1,0:T(8,128)(2,1)} %nh_hbm.1) | copy-start | bytes 6291460
  2.9 1.0 %copy-start.1 = (bf16[256,1024]{1,0:T(8,128)(2,1)S(1)}, bf16[256,1024]{1,0:T(8,128)(2,1)}, u32[]{:S(2)}) copy-start(bf16[256,1024]{1,0:T(8,128)(2,1)} %nf_hbm.1) | copy-start | bytes 1572868
  3.9 1.0 %copy-start.2 = (bf16[256,1024]{1,0:T(8,128)(2,1)S(1)}, bf16[256,1024]{1,0:T(8,128)(2,1)}, u32[]{:S(2)}) copy-start(bf16[256,1024]{1,0:T(8,128)(2,1)} %ef_hbm.1) | copy-start | bytes 1572868
  5.0 0.7 copy-start.3
  5.6 0.7 copy-start.4

commit v2 on v1

v2 whole, which is shorter than its diff:
```python
import functools

import jax
import jax.numpy as jnp
from jax import lax
from jax.experimental import pallas as pl
from jax.experimental.pallas import tpu as pltpu
from jax.sharding import PartitionSpec as P

SHARED = 4
Z = 4
CORES = 2
X = 4
BLOCK = SHARED * Z
MESH = pl.DeviceIdType.MESH
NT = (((1,), (1,)), ((), ()))
TN = (((0,), (0,)), ((), ()))


def dot(a, b, dims=(((1,), (0,)), ((), ()))):
    return lax.dot_general(a, b, dims, preferred_element_type=jnp.float32)


def terms(margins):
    t = jnp.exp(-jnp.abs(margins))
    r = 1.0 / (1.0 + t)
    return jnp.maximum(margins, 0.0) + jnp.log1p(t), jnp.where(margins >= 0.0, r, t * r)


def upper_half(shape):
    return lax.broadcasted_iota(jnp.int32, shape, 0) < SHARED


def pack(rows):
    w = rows.shape[1] // 4
    c = [rows[:, q * w : (q + 1) * w] for q in range(4)]
    up = upper_half(c[0].shape)
    lo = jnp.where(up, c[0], pltpu.roll(c[1], SHARED, 0))
    hi = jnp.where(up, c[2], pltpu.roll(c[3], SHARED, 0))
    return jnp.concatenate([lo, hi], axis=0)


def unpack_pair(first, second):
    up = upper_half((8, first.shape[1]))
    out = []
    for half in range(2):
        a, b = first[half * 8 : half * 8 + 8], second[half * 8 : half * 8 + 8]
        out.append(jnp.where(up, a, pltpu.roll(b, SHARED, 0)))
        out.append(jnp.where(up, pltpu.roll(a, SHARED, 0), b))
    return jnp.concatenate(out, axis=1)


def kernel(
    n_loop, ring,
    nf_hbm, ef_hbm, nh_hbm, eh_hbm, scale_hbm, table_hbm, index_hbm,
    loss_hbm, ng_hbm, eg_hbm,
    nf, ef, nh, eh, scale_ref, table_ref, index_ref, nu, ru, ninv, rinv, ne, re, off, off_out,
    pieces_a, pieces_b, own_piece, W, G, S, R, back_out, back, back_sum, slopes, local_slopes,
    lossacc, loss_out, loss_in, rup, rup_out, rup_in, nup, pre, ng, eg, loss_ref,
    load_sem, store_sem, piece_send, recv_a, recv_b, ag_send, ag_recv, rs_send, rs_recv,
    back_send, back_recv, sib_send, sib_recv,
):
    pairs, width = nf.shape
    tile = min(256, width)
    tiles = width // tile
    l, o = lax.axis_index("loop"), lax.axis_index("outer")
    c, z, y = lax.rem(o, CORES), lax.rem(o // CORES, Z), o // (CORES * Z)
    x = lax.rem(l, X)
    z_first = lax.rem((x + 1) // 2, 2) == 0
    side_a = x // 2
    side_b = 1 - side_a
    pod_a = lax.rem(l + n_loop - 1 + 2 * side_a, n_loop)
    pod_b = lax.rem(l + n_loop + 1 - 2 * side_a, n_loop)

    def outer(yy, zz, cc):
        return (yy * Z + zz) * CORES + cc

    below, above = lax.rem(l + n_loop - 1, n_loop), lax.rem(l + 1, n_loop)
    ys = [lax.rem(y + d, ring) for d in range(ring)]
    zs = [lax.rem(z + d, Z) for d in range(Z)]
    ys_back = [lax.rem(y + ring - d, ring) for d in range(ring)]
    zs_back = [lax.rem(z + Z - d, Z) for d in range(Z)]
    sibling = (l, outer(y, z, 1 - c))

    barrier = pltpu.get_barrier_semaphore()
    partners = [sibling]
    partners += [(l, outer(yy, z, c)) for yy in ys[1:]] + [(l, outer(y, zz, c)) for zz in zs[1:]]
    for pod in (below, above):
        partners += [(pod, outer(yy, z, c)) for yy in ys] + [(pod, outer(y, zz, c)) for zz in zs[1:]]
    for partner in partners:
        pl.semaphore_signal(barrier, inc=1, device_id=partner, device_id_type=MESH)

    loads = [
        pltpu.make_async_copy(src, dst, load_sem.at[i])
        for i, (src, dst) in enumerate((
            (nh_hbm, nh), (nf_hbm, nf), (eh_hbm, eh), (ef_hbm, ef),
            (scale_hbm, scale_ref), (table_hbm, table_ref), (index_hbm, index_ref),
        ))
    ]
    for load in loads:
        load.start()

    def remote(src, dst, send, recv, device):
        return pltpu.make_async_remote_copy(
            src_ref=src, dst_ref=dst, send_sem=send, recv_sem=recv, device_id=device, device_id_type=MESH
        )

    def project(feats, head, unit):
        def step(j, carry):
            cols = pl.ds(pl.multiple_of(j * tile, tile), tile)
            unit[:, cols] = dot(feats[...], head[:, cols])
            return carry

        lax.fori_loop(0, tiles, step, 0)

    def normalise(unit, inverse, emb):
        step_rows = min(64, pairs)

        def step(j, carry):
            rows = pl.ds(pl.multiple_of(j * step_rows, step_rows), step_rows)
            p = unit[rows, :]
            inv = lax.rsqrt(jnp.sum(p * p, axis=-1, keepdims=True) + 1e-06)
            u = p * inv
            inverse[rows, :] = inv
            unit[rows, :] = u
            emb[rows, :] = u.astype(jnp.bfloat16)
            return carry

        lax.fori_loop(0, pairs // step_rows, step, 0)

    loads[0].wait()
    loads[1].wait()
    project(nf, nh, nu)
    top = nu[0:8, :]
    top = top * lax.rsqrt(jnp.sum(top * top, axis=-1, keepdims=True) + 1e-06)
    own_piece[...] = pack(top).astype(jnp.bfloat16)
    pl.semaphore_wait(barrier, len(partners))

    def piece_sends(along_z):
        copies = []
        for side, pod in enumerate((above, below)):
            for d in range(Z if along_z else ring):
                device = (pod, outer(y, zs[d], c) if along_z else outer(ys[d], z, c))
                landing, recv = (pieces_a, recv_a) if along_z else (pieces_b, recv_b)
                copies.append(
                    remote(own_piece, landing.at[d], piece_send.at[side * ring + d], recv.at[d], device)
                )
        return copies

    @pl.when(z_first)
    def _():
        for copy in piece_sends(True):
            copy.start()

    @pl.when(jnp.logical_not(z_first))
    def _():
        for copy in piece_sends(False):
            copy.start()

    normalise(nu, ninv, ne)

    for load in loads[2:]:
        load.wait()
    project(ef, eh, ru)
    normalise(ru, rinv, re.at[pl.ds(0, pairs)])
    index = index_ref[...]
    offsets = jnp.zeros(index.shape, jnp.float32)
    for k in range(table_ref.shape[0]):
        offsets = jnp.where(index == k, table_ref[k], offsets)
    off_out[...] = jnp.broadcast_to(offsets, off_out.shape)
    sib_rec = remote(re.at[pl.ds(0, pairs)], re.at[pl.ds(pairs, pairs)], sib_send.at[0], sib_recv.at[0], sibling)
    sib_off = remote(off_out, off, sib_send.at[1], sib_recv.at[1], sibling)
    sib_rec.start()
    sib_off.start()
    scale = scale_ref[0]

    rows_a, rows_b = BLOCK, SHARED * ring
    groups = [[("a", 0), ("b", 0)], [], [], []]
    for dist in range(1, ring // 2 + 1):
        groups[min(dist, 3)] += [("a", d) for d in sorted({dist, ring - dist})]
    for group, d in ((1, 1), (2, 3), (3, 2)):
        groups[group].append(("b", d))
    place, spans, first = {}, [], 0
    for group in groups:
        start = first
        for kind, d in group:
            size = rows_a if kind == "a" else rows_b
            place[kind, d] = (first, size)
            first += size
        spans.append((start, first))
    sem_of = {key: i for i, key in enumerate(k for k in place if k[1])}

    def gather(kind, d):
        (src, size), (dst, _) = place[kind, 0], place[kind, d]
        i = sem_of[kind, d]
        device = (l, outer(ys[d], z, c)) if kind == "a" else (l, outer(y, zs[d], c))
        return remote(W.at[pl.ds(src, size)], W.at[pl.ds(dst, size)], ag_send.at[i], ag_recv.at[i], device)

    def give_back(kind, d):
        rows = pl.ds(*place[kind, d])
        i = sem_of[kind, d]
        device = (l, outer(ys_back[d], z, c)) if kind == "a" else (l, outer(y, zs_back[d], c))
        return remote(S.at[rows], R.at[rows], rs_send.at[i], rs_recv.at[i], device)

    gathers = {key: gather(*key) for key in sem_of}
    reduces = {key: give_back(*key) for key in sem_of}

    def collect(kind, landing, recv, count):
        for d in range(count):
            remote(own_piece, landing.at[d], piece_send.at[0], recv.at[d], sibling).wait_recv()
        p = [landing[d].astype(jnp.float32) for d in range(count)]
        block = jnp.concatenate([unpack_pair(p[d], p[d + 1]) for d in range(0, count, 2)], axis=0)
        start, size = place[kind, 0]
        W[start : start + size, :] = block.astype(jnp.bfloat16)
        for key in sem_of:
            if key[0] == kind:
                gathers[key].start()

    sims = dot(ne[...], re[0:pairs, :], NT)
    logits = scale * sims + offsets
    positive = lax.broadcasted_iota(jnp.int32, logits.shape, 0) == lax.broadcasted_iota(jnp.int32, logits.shape, 1)
    softplus, sigmoid = terms(jnp.where(positive, -logits, logits))
    local_slopes[...] = jnp.where(positive, -sigmoid, sigmoid).astype(jnp.bfloat16)
    lossacc[:, 0:pairs] = jnp.sum(softplus.reshape(pairs // 8, 8, pairs), axis=0)
    lossacc[:, pairs:] = jnp.zeros((8, pairs), jnp.float32)

    collect("b", pieces_b, recv_b, ring)
    collect("a", pieces_a, recv_a, Z)

    def back_grad(head, out):
        def step(j, carry):
            cols = pl.ds(pl.multiple_of(j * tile, tile), tile)
            out[:, cols] = dot(pre[...], head[cols, :], NT)
            return carry

        lax.fori_loop(0, tiles, step, 0)

    def pre_grads(unit, inverse, upstream):
        step_rows = min(64, pairs)

        def step(j, carry):
            rows = pl.ds(pl.multiple_of(j * step_rows, step_rows), step_rows)
            u, up = unit[rows, :], upstream(rows)
            radial = jnp.sum(u * up, axis=-1, keepdims=True)
            pre[rows, :] = (inverse[rows, :] * (up - u * radial)).astype(jnp.bfloat16)
            return carry

        lax.fori_loop(0, pairs // step_rows, step, 0)

    sib_off.wait_recv()
    sib_rec.wait_recv()
    all_offsets = jnp.concatenate([off_out[0:1, :], off[0:1, :]], axis=1)

    def work(g):
        for key in groups[g]:
            if key[1]:
                gathers[key].wait_recv()
        start, stop = spans[g]
        n = stop - start
        if n == 0:
            return
        logits = scale * dot(W[start:stop, :], re[...], NT) + all_offsets
        softplus, sigmoid = terms(logits)
        lossacc[...] += jnp.sum(softplus.reshape(n // 8, 8, 2 * pairs), axis=0)
        s = sigmoid.astype(jnp.bfloat16)
        slopes[start:stop, :] = s
        grads = dot(s, re[...])
        if g == 0:
            G[...] = grads
        else:
            S[start:stop, :] = grads.astype(jnp.bfloat16)
            for key in groups[g]:
                reduces[key].start()

    work(0)

    def upstream_notes(j, carry):
        cols = pl.ds(pl.multiple_of(j * tile, tile), tile)
        nup[:, cols] = scale * dot(local_slopes[...], re[0:pairs, cols])
        return carry

    lax.fori_loop(0, tiles, upstream_notes, 0)
    pre_grads(nu, ninv, lambda rows: nup[rows, :])
    back_grad(nh, ng)
    stores = [
        pltpu.make_async_copy(ng.at[pl.ds(8, pairs - 8)], ng_hbm.at[pl.ds(8, pairs - 8)], store_sem.at[0]),
        pltpu.make_async_copy(eg, eg_hbm, store_sem.at[1]),
        pltpu.make_async_copy(loss_ref, loss_hbm, store_sem.at[2]),
        pltpu.make_async_copy(ng.at[pl.ds(0, 8)], ng_hbm.at[pl.ds(0, 8)], store_sem.at[3]),
    ]
    stores[0].start()
    for g in (1, 2, 3):
        work(g)

    def upstream_sibling(j, carry):
        cols = pl.ds(pl.multiple_of(j * tile, tile), tile)
        rup_out[:, cols] = dot(slopes[:, pairs:], W[:, cols], TN)
        return carry

    def upstream_own(j, carry):
        cols = pl.ds(pl.multiple_of(j * tile, tile), tile)
        rup[:, cols] = dot(slopes[:, 0:pairs], W[:, cols], TN) + dot(local_slopes[...], ne[:, cols], TN)
        return carry

    lax.fori_loop(0, tiles, upstream_sibling, 0)
    loss_out[...] = lossacc[:, pairs:]
    sib_rup = remote(rup_out, rup_in, sib_send.at[2], sib_recv.at[2], sibling)
    sib_loss = remote(loss_out, loss_in, sib_send.at[3], sib_recv.at[3], sibling)
    sib_rup.start()
    sib_loss.start()
    lax.fori_loop(0, tiles, upstream_own, 0)
    sib_rup.wait_recv()
    sib_loss.wait_recv()
    loss = jnp.sum(lossacc[:, 0:pairs] + loss_in[...], axis=0, keepdims=True)
    loss_ref[...] = loss * (1.0 / (pairs + ring * Z * CORES * SHARED * 2))
    pre_grads(ru, rinv, lambda rows: scale * (rup[rows, :] + rup_in[rows, :]))
    back_grad(eh, eg)
    stores[1].start()
    stores[2].start()

    returns = []
    for kind, pod, side, count in (("b", pod_b, side_b, ring), ("a", pod_a, side_a, Z)):
        start, size = place[kind, 0]
        total = G[start : start + size, :]
        for key in sem_of:
            if key[0] == kind:
                reduces[key].wait_recv()
                first, _ = place[key]
                total = total + R[first : first + size, :].astype(jnp.float32)
        total = scale * total
        for d in range(count):
            half = total[(d // 2) * 8 : (d // 2) * 8 + 8, :]
            if d % 2:
                half = pltpu.roll(half, SHARED, 0)
            i = d + (Z if kind == "b" else 0)
            back_out[i] = pack(half).astype(jnp.bfloat16)
            owner = outer(ys_back[d], z, c) if kind == "b" else outer(y, zs_back[d], c)
            k = side * ring + d
            copy = remote(back_out.at[i], back.at[k], back_send.at[i], back_recv.at[k], (pod, owner))
            copy.start()
            returns.append(copy)

    def take_back(count):
        total = None
        for side in range(2):
            for d in range(count):
                k = side * ring + d
                remote(own_piece, back.at[k], back_send.at[0], back_recv.at[k], sibling).wait_recv()
                part = back[k].astype(jnp.float32)
                total = part if total is None else total + part
        back_sum[...] = total

    @pl.when(z_first)
    def _():
        take_back(Z)

    @pl.when(jnp.logical_not(z_first))
    def _():
        take_back(ring)

    lo, hi = back_sum[0:8, :], back_sum[8:16, :]
    spread = jnp.concatenate([lo, pltpu.roll(lo, SHARED, 0), hi, pltpu.roll(hi, SHARED, 0)], axis=1)
    up = nup[0:8, :] + jnp.where(upper_half(spread.shape), spread, 0.0)
    u = nu[0:8, :]
    radial = jnp.sum(u * up, axis=-1, keepdims=True)
    g = (ninv[0:8, :] * (up - u * radial)).astype(jnp.bfloat16)
    ng[0:8, :] = dot(g, nh[...], NT)
    stores[3].start()

    @pl.when(z_first)
    def _():
        for copy in piece_sends(True):
            copy.wait_send()

    @pl.when(jnp.logical_not(z_first))
    def _():
        for copy in piece_sends(False):
            copy.wait_send()

    for copy in list(gathers.values()) + list(reduces.values()) + returns:
        copy.wait_send()
    for copy in (sib_rec, sib_off, sib_rup, sib_loss):
        copy.wait_send()
    for copy in stores:
        copy.wait()


def write_out(loss_in, ng_in, eg_in, loss_out, ng_out, eg_out, loss, ng, eg, in_sem, out_sem):
    parts = 4
    rows = ng.shape[0] // parts
    moves = [(loss_in, loss, loss_out)]
    for src, held, dst in ((ng_in, ng, ng_out), (eg_in, eg, eg_out)):
        for j in range(parts):
            part = pl.ds(j * rows, rows)
            moves.append((src.at[part], held.at[part], dst.at[part]))
    loads = [pltpu.make_async_copy(src, held, in_sem.at[i]) for i, (src, held, _) in enumerate(moves)]
    stores = [pltpu.make_async_copy(held, dst, out_sem.at[i]) for i, (_, held, dst) in enumerate(moves)]
    for load in loads:
        load.start()
    for load, store in zip(loads, stores):
        load.wait()
        store.start()
    for store in stores:
        store.wait()


def per_device(n_loop, n_outer, note_feats, ehr_feats, note_head, ehr_head, logit_scale, bias_table, bias_index):
    pairs, width = note_feats.shape
    emb = note_head.shape[1]
    ring = n_outer // (Z * CORES)
    held = 2 * ring * BLOCK
    own = BLOCK + SHARED * ring
    others = ring + Z - 2
    bf16, f32 = jnp.bfloat16, jnp.float32
    vmem = pltpu.VMEM
    dma = pltpu.SemaphoreType.DMA
    hbm = pl.BlockSpec(memory_space=pltpu.HBM)
    outs = (
        jax.ShapeDtypeStruct((1, pairs), f32),
        jax.ShapeDtypeStruct((pairs, width), f32),
        jax.ShapeDtypeStruct((pairs, width), f32),
    )
    piece = (BLOCK, emb // 4)
    results = pl.pallas_call(
        functools.partial(kernel, n_loop, ring),
        out_shape=outs,
        in_specs=[hbm] * 7,
        out_specs=(hbm,) * 3,
        scratch_shapes=[
            vmem((pairs, width), bf16),
            vmem((pairs, width), bf16),
            vmem((width, emb), bf16),
            vmem((width, emb), bf16),
            pltpu.SMEM(logit_scale.shape, f32),
            pltpu.SMEM(bias_table.shape, f32),
            vmem((1, pairs), jnp.int32),
            vmem((pairs, emb), f32),
            vmem((pairs, emb), f32),
            vmem((pairs, 1), f32),
            vmem((pairs, 1), f32),
            vmem((pairs, emb), bf16),
            vmem((2 * pairs, emb), bf16),
            vmem((8, pairs), f32),
            vmem((8, pairs), f32),
            vmem((Z,) + piece, bf16),
            vmem((ring,) + piece, bf16),
            vmem(piece, bf16),
            vmem((held, emb), bf16),
            vmem((own, emb), f32),
            vmem((held, emb), bf16),
            vmem((held, emb), bf16),
            vmem((Z + ring,) + piece, bf16),
            vmem((2 * ring,) + piece, bf16),
            vmem(piece, f32),
            vmem((held, 2 * pairs), bf16),
            vmem((pairs, pairs), bf16),
            vmem((8, 2 * pairs), f32),
            vmem((8, pairs), f32),
            vmem((8, pairs), f32),
            vmem((pairs, emb), f32),
            vmem((pairs, emb), f32),
            vmem((pairs, emb), f32),
            vmem((pairs, emb), f32),
            vmem((pairs, emb), bf16),
            vmem((pairs, width), f32),
            vmem((pairs, width), f32),
            vmem((1, pairs), f32),
            dma((7,)),
            dma((4,)),
            dma((2 * ring,)),
            dma((Z,)),
            dma((ring,)),
            dma((others,)),
            dma((others,)),
            dma((others,)),
            dma((others,)),
            dma((Z + ring,)),
            dma((2 * ring,)),
            dma((4,)),
            dma((4,)),
        ],
        compiler_params=pltpu.CompilerParams(
            collective_id=0, has_side_effects=True, vmem_limit_bytes=56 * 1024 * 1024
        ),
    )(note_feats, ehr_feats, note_head, ehr_head, logit_scale, bias_table, bias_index.reshape(1, pairs))
    loss, note_grad, ehr_grad = pl.pallas_call(
        write_out,
        out_shape=outs,
        in_specs=[hbm] * 3,
        out_specs=(hbm,) * 3,
        scratch_shapes=[vmem(out.shape, f32) for out in outs] + [dma((9,)), dma((9,))],
        compiler_params=pltpu.CompilerParams(vmem_limit_bytes=62 * 1024 * 1024),
    )(*results)
    return loss.reshape(pairs), note_grad, ehr_grad


def solution(mesh):
    return jax.shard_map(
        functools.partial(per_device, mesh.shape["loop"], mesh.shape["outer"]),
        mesh=mesh,
        in_specs=(
            P(("loop", "outer"), None),
            P(("loop", "outer"), None),
            P(),
            P(),
            P(),
            P(),
            P(("loop", "outer")),
        ),
        out_specs=(P(("loop", "outer")), P(("loop", "outer"), None), P(("loop", "outer"), None)),
        check_vma=False,
    )
```

time: 70.4 us -> 55.2 us (0.78)
  the two profiles are of different devices: /device:TPU:8 before, /device:TPU:64 now
where the time goes in v2:
time: 55.2 us; the launch traced here: 54.8 us
  Pallas kernels  53.5 us (97%)
  between operations  1.29 us (2%)
    pallas_call x1, Pallas kernels, per_device(): pl.pallas_call(functools.partial(kernel, n_loop, ring), out_shape=outs, i...  51.1 us
    pallas_call x1, Pallas kernels, per_device(): pl.pallas_call(write_out, out_shape=outs, in_specs=[hbm] * 3, out_specs=(...  2.42 us

profile of v2, /device:TPU:64, one launch (start us, length us, event | category | flops | bytes accessed | tf_op | source)
XLA Modules:
  0.0 54.8 jit_solution(5510786672211296544)
XLA Ops:
  1.3 51.1 %shard_map.94 = (f32[1,256]{1,0:T(1,128)}, f32[256,1024]{1,0:T(8,128)}, f32[256,1024]{1,0:T(8,128)}) custom-call(bf16[256,1024]{1,0:T(8,128)(2,1)} %nf_hbm.1, bf16[256,1024]{1,0:T(8,128)(2,1)} %ef_hbm.1, bf16[1024,1024]{1,0:T(8,128)(2,1)} %nh_hbm.1, bf16[1024,1024]{1,0:T(8,128)(2,1)} %eh_hbm.1, f32[1]{0:T(128)S(6)} %copy.10.scale_hbm, f32[16]{0:T(128)} %table_hbm.1, ...), custom_call_target="tpu_custom_call" | custom-call | tf_op jit(solution)/shard_map/pallas_call | solution.py:424
  52.3 2.4 %shard_map.95 = (f32[1,256]{1,0:T(1,128)}, f32[256,1024]{1,0:T(8,128)}, f32[256,1024]{1,0:T(8,128)}) custom-call(f32[1,256]{1,0:T(1,128)} %get-tuple-element.9.loss_in, f32[256,1024]{1,0:T(8,128)} %get-tuple-element.10.ng_in, f32[256,1024]{1,0:T(8,128)} %get-tuple-element.11.eg_in), custom_call_target="tpu_custom_call" | custom-call | tf_op jit(solution)/shard_map/pallas_call | solution.py:486

commit v3 on v2

--- a/solution.py
+++ b/solution.py
@@ -11,6 +11,7 @@
 Z = 4
 CORES = 2
 X = 4
+HEAD_PARTS = 4
 BLOCK = SHARED * Z
 MESH = pl.DeviceIdType.MESH
 NT = (((1,), (1,)), ((), ()))
@@ -53,11 +54,13 @@
 def kernel(
     n_loop, ring,
     nf_hbm, ef_hbm, nh_hbm, eh_hbm, scale_hbm, table_hbm, index_hbm,
-    loss_hbm, ng_hbm, eg_hbm,
+    loss_ref, ng, eg,
     nf, ef, nh, eh, scale_ref, table_ref, index_ref, nu, ru, ninv, rinv, ne, re, off, off_out,
-    pieces_a, pieces_b, own_piece, W, G, S, R, back_out, back, back_sum, slopes, local_slopes,
-    lossacc, loss_out, loss_in, rup, rup_out, rup_in, nup, pre, ng, eg, loss_ref,
-    load_sem, store_sem, piece_send, recv_a, recv_b, ag_send, ag_recv, rs_send, rs_recv,
+    pieces_a, pieces_b, own_piece, W, G, S, R, held_a, own_a, sent_a, came_a, back_out, back, back_sum,
+    slopes, local_slopes,
+    lossacc, loss_out, loss_in, rup, rup_out, rup_in, nup, pre,
+    load_sem, piece_send, recv_a, recv_b, ag_send, ag_recv, rs_send, rs_recv,
+    fwd_send, fwd_recv, sum_send, sum_recv,
     back_send, back_recv, sib_send, sib_recv,
 ):
     pairs, width = nf.shape
@@ -90,13 +93,17 @@
     for partner in partners:
         pl.semaphore_signal(barrier, inc=1, device_id=partner, device_id_type=MESH)
 
-    loads = [
-        pltpu.make_async_copy(src, dst, load_sem.at[i])
-        for i, (src, dst) in enumerate((
-            (nh_hbm, nh), (nf_hbm, nf), (eh_hbm, eh), (ef_hbm, ef),
-            (scale_hbm, scale_ref), (table_hbm, table_ref), (index_hbm, index_ref),
-        ))
+    top_rows, deep = pl.ds(0, 16), nh.shape[0] // HEAD_PARTS
+    other_rows = pl.ds(16, pairs - 16)
+    moves = [(nf_hbm.at[top_rows], nf.at[top_rows])]
+    for j in range(HEAD_PARTS):
+        part = pl.ds(j * deep, deep)
+        moves.append((nh_hbm.at[part], nh.at[part]))
+    moves += [
+        (nf_hbm.at[other_rows], nf.at[other_rows]), (eh_hbm, eh), (ef_hbm, ef),
+        (scale_hbm, scale_ref), (table_hbm, table_ref), (index_hbm, index_ref),
     ]
+    loads = [pltpu.make_async_copy(src, dst, load_sem.at[i]) for i, (src, dst) in enumerate(moves)]
     for load in loads:
         load.start()
 
@@ -128,8 +135,8 @@
 
         lax.fori_loop(0, pairs // step_rows, step, 0)
 
-    loads[0].wait()
-    loads[1].wait()
+    for load in loads[: 2 + HEAD_PARTS]:
+        load.wait()
     project(nf, nh, nu)
     top = nu[0:8, :]
     top = top * lax.rsqrt(jnp.sum(top * top, axis=-1, keepdims=True) + 1e-06)
@@ -159,7 +166,7 @@
 
     normalise(nu, ninv, ne)
 
-    for load in loads[2:]:
+    for load in loads[2 + HEAD_PARTS :]:
         load.wait()
     project(ef, eh, ru)
     normalise(ru, rinv, re.at[pl.ds(0, pairs)])
@@ -174,47 +181,44 @@
     sib_off.start()
     scale = scale_ref[0]
 
-    rows_a, rows_b = BLOCK, SHARED * ring
-    groups = [[("a", 0), ("b", 0)], [], [], []]
-    for dist in range(1, ring // 2 + 1):
-        groups[min(dist, 3)] += [("a", d) for d in sorted({dist, ring - dist})]
-    for group, d in ((1, 1), (2, 3), (3, 2)):
-        groups[group].append(("b", d))
-    place, spans, first = {}, [], 0
-    for group in groups:
-        start = first
-        for kind, d in group:
-            size = rows_a if kind == "a" else rows_b
-            place[kind, d] = (first, size)
-            first += size
-        spans.append((start, first))
-    sem_of = {key: i for i, key in enumerate(k for k in place if k[1])}
-
-    def gather(kind, d):
-        (src, size), (dst, _) = place[kind, 0], place[kind, d]
-        i = sem_of[kind, d]
-        device = (l, outer(ys[d], z, c)) if kind == "a" else (l, outer(y, zs[d], c))
-        return remote(W.at[pl.ds(src, size)], W.at[pl.ds(dst, size)], ag_send.at[i], ag_recv.at[i], device)
-
-    def give_back(kind, d):
-        rows = pl.ds(*place[kind, d])
-        i = sem_of[kind, d]
-        device = (l, outer(ys_back[d], z, c)) if kind == "a" else (l, outer(y, zs_back[d], c))
-        return remote(S.at[rows], R.at[rows], rs_send.at[i], rs_recv.at[i], device)
-
-    gathers = {key: gather(*key) for key in sem_of}
-    reduces = {key: give_back(*key) for key in sem_of}
-
-    def collect(kind, landing, recv, count):
-        for d in range(count):
-            remote(own_piece, landing.at[d], piece_send.at[0], recv.at[d], sibling).wait_recv()
-        p = [landing[d].astype(jnp.float32) for d in range(count)]
-        block = jnp.concatenate([unpack_pair(p[d], p[d + 1]) for d in range(0, count, 2)], axis=0)
-        start, size = place[kind, 0]
-        W[start : start + size, :] = block.astype(jnp.bfloat16)
-        for key in sem_of:
-            if key[0] == kind:
-                gathers[key].start()
+    size = SHARED * ring
+    far_first = sorted(range(1, ring), key=lambda d: -min(d, ring - d))
+
+    def rows_b(d):
+        return pl.ds(size * (Z + d), size)
+
+    def forward(p, d):
+        i = p * ring + d
+        return remote(pieces_a.at[p], held_a.at[i], fwd_send.at[i], fwd_recv.at[i], (l, outer(ys[d], z, c)))
+
+    def sum_a(p, d):
+        i = p * ring + d
+        return remote(sent_a.at[i], came_a.at[i], sum_send.at[i], sum_recv.at[i], (l, outer(ys_back[d], z, c)))
+
+    forwards = {(p, d): forward(p, d) for p in range(Z) for d in far_first}
+    sums_a = {(p, d): sum_a(p, d) for p in range(Z) for d in far_first}
+    gathers, reduces = {}, {}
+    for d in range(1, Z):
+        gathers[d] = remote(
+            W.at[rows_b(0)], W.at[rows_b(d)], ag_send.at[d], ag_recv.at[d], (l, outer(y, zs[d], c))
+        )
+        reduces[d] = remote(
+            S.at[pl.ds(size * d, size)], R.at[pl.ds(size * d, size)], rs_send.at[d], rs_recv.at[d],
+            (l, outer(y, zs_back[d], c)),
+        )
+
+    def unpacked(packed):
+        return jnp.concatenate([unpack_pair(packed[d], packed[d + 1]) for d in range(0, len(packed), 2)], axis=0)
+
+    for p in range(Z):
+        remote(own_piece, pieces_a.at[p], piece_send.at[0], recv_a.at[p], sibling).wait_recv()
+        for d in far_first:
+            forwards[p, d].start()
+    for d in range(ring):
+        remote(own_piece, pieces_b.at[d], piece_send.at[0], recv_b.at[d], sibling).wait_recv()
+    W[rows_b(0), :] = unpacked([pieces_b[d].astype(jnp.float32) for d in range(ring)]).astype(jnp.bfloat16)
+    for d in (2, 1, 3):
+        gathers[d].start()
 
     sims = dot(ne[...], re[0:pairs, :], NT)
     logits = scale * sims + offsets
@@ -224,9 +228,6 @@
     lossacc[:, 0:pairs] = jnp.sum(softplus.reshape(pairs // 8, 8, pairs), axis=0)
     lossacc[:, pairs:] = jnp.zeros((8, pairs), jnp.float32)
 
-    collect("b", pieces_b, recv_b, ring)
-    collect("a", pieces_a, recv_a, Z)
-
     def back_grad(head, out):
         def step(j, carry):
             cols = pl.ds(pl.multiple_of(j * tile, tile), tile)
@@ -251,28 +252,37 @@
     sib_rec.wait_recv()
     all_offsets = jnp.concatenate([off_out[0:1, :], off[0:1, :]], axis=1)
 
-    def work(g):
-        for key in groups[g]:
-            if key[1]:
-                gathers[key].wait_recv()
-        start, stop = spans[g]
-        n = stop - start
-        if n == 0:
-            return
-        logits = scale * dot(W[start:stop, :], re[...], NT) + all_offsets
+    def work(start):
+        rows = slice(start, start + size)
+        logits = scale * dot(W[rows, :], re[...], NT) + all_offsets
         softplus, sigmoid = terms(logits)
-        lossacc[...] += jnp.sum(softplus.reshape(n // 8, 8, 2 * pairs), axis=0)
+        lossacc[...] += jnp.sum(softplus.reshape(size // 8, 8, 2 * pairs), axis=0)
         s = sigmoid.astype(jnp.bfloat16)
-        slopes[start:stop, :] = s
-        grads = dot(s, re[...])
-        if g == 0:
-            G[...] = grads
-        else:
-            S[start:stop, :] = grads.astype(jnp.bfloat16)
-            for key in groups[g]:
-                reduces[key].start()
-
-    work(0)
+        slopes[rows, :] = s
+        return dot(s, re[...])
+
+    def work_b(d):
+        gathers[d].wait_recv()
+        S[pl.ds(size * d, size), :] = work(size * (Z + d)).astype(jnp.bfloat16)
+        reduces[d].start()
+
+    def work_a(p):
+        for d in far_first:
+            forwards[p, d].wait_recv()
+        packed = [pieces_a[p]] + [held_a[p * ring + d] for d in range(1, ring)]
+        W[size * p : size * (p + 1), :] = unpacked([q.astype(jnp.float32) for q in packed]).astype(jnp.bfloat16)
+        grads = work(size * p)
+        for d in [0] + far_first:
+            half = grads[(d // 2) * 8 : (d // 2) * 8 + 8, :]
+            if d % 2:
+                half = pltpu.roll(half, SHARED, 0)
+            if d == 0:
+                own_a[p] = pack(half)
+            else:
+                sent_a[p * ring + d] = pack(half).astype(jnp.bfloat16)
+                sums_a[p, d].start()
+
+    G[...] = work(size * Z)
 
     def upstream_notes(j, carry):
         cols = pl.ds(pl.multiple_of(j * tile, tile), tile)
@@ -282,15 +292,13 @@
     lax.fori_loop(0, tiles, upstream_notes, 0)
     pre_grads(nu, ninv, lambda rows: nup[rows, :])
     back_grad(nh, ng)
-    stores = [
-        pltpu.make_async_copy(ng.at[pl.ds(8, pairs - 8)], ng_hbm.at[pl.ds(8, pairs - 8)], store_sem.at[0]),
-        pltpu.make_async_copy(eg, eg_hbm, store_sem.at[1]),
-        pltpu.make_async_copy(loss_ref, loss_hbm, store_sem.at[2]),
-        pltpu.make_async_copy(ng.at[pl.ds(0, 8)], ng_hbm.at[pl.ds(0, 8)], store_sem.at[3]),
-    ]
-    stores[0].start()
-    for g in (1, 2, 3):
-        work(g)
+    work_a(0)
+    work_b(1)
+    work_a(1)
+    work_b(3)
+    work_a(2)
+    work_b(2)
+    work_a(3)
 
     def upstream_sibling(j, carry):
         cols = pl.ds(pl.multiple_of(j * tile, tile), tile)
@@ -309,36 +317,50 @@
     sib_rup.start()
     sib_loss.start()
     lax.fori_loop(0, tiles, upstream_own, 0)
+
+    returns = []
+
+    def give(i, d, kind):
+        owner = outer(ys_back[d], z, c) if kind == "b" else outer(y, zs_back[d], c)
+        pod, side = (pod_b, side_b) if kind == "b" else (pod_a, side_a)
+        k = side * ring + d
+        copy = remote(back_out.at[i], back.at[k], back_send.at[i], back_recv.at[k], (pod, owner))
+        copy.start()
+        returns.append(copy)
+
+    def return_a(p):
+        total = own_a[p]
+        for d in far_first:
+            sums_a[p, d].wait_recv()
+            total = total + came_a[p * ring + d].astype(jnp.float32)
+        back_out[p] = (scale * total).astype(jnp.bfloat16)
+        give(p, p, "a")
+
+    def return_b():
+        total = G[...]
+        for d in range(1, Z):
+            reduces[d].wait_recv()
+            total = total + R[pl.ds(size * d, size), :].astype(jnp.float32)
+        total = scale * total
+        for d in range(ring):
+            half = total[(d // 2) * 8 : (d // 2) * 8 + 8, :]
+            if d % 2:
+                half = pltpu.roll(half, SHARED, 0)
+            back_out[Z + d] = pack(half).astype(jnp.bfloat16)
+            give(Z + d, d, "b")
+
+    return_a(0)
+    return_a(1)
+    return_b()
+    return_a(2)
+    return_a(3)
+
     sib_rup.wait_recv()
     sib_loss.wait_recv()
     loss = jnp.sum(lossacc[:, 0:pairs] + loss_in[...], axis=0, keepdims=True)
     loss_ref[...] = loss * (1.0 / (pairs + ring * Z * CORES * SHARED * 2))
     pre_grads(ru, rinv, lambda rows: scale * (rup[rows, :] + rup_in[rows, :]))
     back_grad(eh, eg)
-    stores[1].start()
-    stores[2].start()
-
-    returns = []
-    for kind, pod, side, count in (("b", pod_b, side_b, ring), ("a", pod_a, side_a, Z)):
-        start, size = place[kind, 0]
-        total = G[start : start + size, :]
-        for key in sem_of:
-            if key[0] == kind:
-                reduces[key].wait_recv()
-                first, _ = place[key]
-                total = total + R[first : first + size, :].astype(jnp.float32)
-        total = scale * total
-        for d in range(count):
-            half = total[(d // 2) * 8 : (d // 2) * 8 + 8, :]
-            if d % 2:
-                half = pltpu.roll(half, SHARED, 0)
-            i = d + (Z if kind == "b" else 0)
-            back_out[i] = pack(half).astype(jnp.bfloat16)
-            owner = outer(ys_back[d], z, c) if kind == "b" else outer(y, zs_back[d], c)
-            k = side * ring + d
-            copy = remote(back_out.at[i], back.at[k], back_send.at[i], back_recv.at[k], (pod, owner))
-            copy.start()
-            returns.append(copy)
 
     def take_back(count):
         total = None
@@ -365,7 +387,6 @@
     radial = jnp.sum(u * up, axis=-1, keepdims=True)
     g = (ninv[0:8, :] * (up - u * radial)).astype(jnp.bfloat16)
     ng[0:8, :] = dot(g, nh[...], NT)
-    stores[3].start()
 
     @pl.when(z_first)
     def _():
@@ -377,31 +398,26 @@
         for copy in piece_sends(False):
             copy.wait_send()
 
-    for copy in list(gathers.values()) + list(reduces.values()) + returns:
+    rings = list(forwards.values()) + list(sums_a.values())
+    for copy in rings + list(gathers.values()) + list(reduces.values()) + returns:
         copy.wait_send()
     for copy in (sib_rec, sib_off, sib_rup, sib_loss):
         copy.wait_send()
-    for copy in stores:
+
+
+def write_out(loss, ng, eg, loss_out, ng_out, eg_out, sem):
+    copies = [
+        pltpu.make_async_copy(src, dst, sem.at[i])
+        for i, (src, dst) in enumerate(((ng, ng_out), (eg, eg_out), (loss, loss_out)))
+    ]
+    for copy in copies:
+        copy.start()
+    for copy in copies:
         copy.wait()
 
 
-def write_out(loss_in, ng_in, eg_in, loss_out, ng_out, eg_out, loss, ng, eg, in_sem, out_sem):
-    parts = 4
-    rows = ng.shape[0] // parts
-    moves = [(loss_in, loss, loss_out)]
-    for src, held, dst in ((ng_in, ng, ng_out), (eg_in, eg, eg_out)):
-        for j in range(parts):
-            part = pl.ds(j * rows, rows)
-            moves.append((src.at[part], held.at[part], dst.at[part]))
-    loads = [pltpu.make_async_copy(src, held, in_sem.at[i]) for i, (src, held, _) in enumerate(moves)]
-    stores = [pltpu.make_async_copy(held, dst, out_sem.at[i]) for i, (_, held, dst) in enumerate(moves)]
-    for load in loads:
-        load.start()
-    for load, store in zip(loads, stores):
-        load.wait()
-        store.start()
-    for store in stores:
-        store.wait()
+def in_hbm(a):
+    return pltpu.with_memory_space_constraint(a, pltpu.HBM)
 
 
 def per_device(n_loop, n_outer, note_feats, ehr_feats, note_head, ehr_head, logit_scale, bias_table, bias_index):
@@ -409,12 +425,12 @@
     emb = note_head.shape[1]
     ring = n_outer // (Z * CORES)
     held = 2 * ring * BLOCK
-    own = BLOCK + SHARED * ring
-    others = ring + Z - 2
+    own = SHARED * ring
     bf16, f32 = jnp.bfloat16, jnp.float32
     vmem = pltpu.VMEM
     dma = pltpu.SemaphoreType.DMA
     hbm = pl.BlockSpec(memory_space=pltpu.HBM)
+    whole = pl.BlockSpec(memory_space=pltpu.VMEM)
     outs = (
         jax.ShapeDtypeStruct((1, pairs), f32),
         jax.ShapeDtypeStruct((pairs, width), f32),
@@ -423,9 +439,9 @@
     piece = (BLOCK, emb // 4)
     results = pl.pallas_call(
         functools.partial(kernel, n_loop, ring),
-        out_shape=outs,
+        out_shape=tuple(vmem(out.shape, f32) for out in outs),
         in_specs=[hbm] * 7,
-        out_specs=(hbm,) * 3,
+        out_specs=(whole,) * 3,
         scratch_shapes=[
             vmem((pairs, width), bf16),
             vmem((pairs, width), bf16),
@@ -447,8 +463,12 @@
             vmem(piece, bf16),
             vmem((held, emb), bf16),
             vmem((own, emb), f32),
-            vmem((held, emb), bf16),
-            vmem((held, emb), bf16),
+            vmem((held // 2, emb), bf16),
+            vmem((held // 2, emb), bf16),
+            vmem((Z * ring,) + piece, bf16),
+            vmem((Z,) + piece, f32),
+            vmem((Z * ring,) + piece, bf16),
+            vmem((Z * ring,) + piece, bf16),
             vmem((Z + ring,) + piece, bf16),
             vmem((2 * ring,) + piece, bf16),
             vmem(piece, f32),
@@ -462,34 +482,37 @@
             vmem((pairs, emb), f32),
             vmem((pairs, emb), f32),
             vmem((pairs, emb), bf16),
-            vmem((pairs, width), f32),
-            vmem((pairs, width), f32),
-            vmem((1, pairs), f32),
-            dma((7,)),
-            dma((4,)),
+            dma((7 + HEAD_PARTS,)),
             dma((2 * ring,)),
             dma((Z,)),
             dma((ring,)),
-            dma((others,)),
-            dma((others,)),
-            dma((others,)),
-            dma((others,)),
+            dma((Z,)),
+            dma((Z,)),
+            dma((Z,)),
+            dma((Z,)),
+            dma((Z * ring,)),
+            dma((Z * ring,)),
+            dma((Z * ring,)),
+            dma((Z * ring,)),
             dma((Z + ring,)),
             dma((2 * ring,)),
             dma((4,)),
             dma((4,)),
         ],
         compiler_params=pltpu.CompilerParams(
-            collective_id=0, has_side_effects=True, vmem_limit_bytes=56 * 1024 * 1024
+            collective_id=0, has_side_effects=True, vmem_limit_bytes=48 * 1024 * 1024
         ),
-    )(note_feats, ehr_feats, note_head, ehr_head, logit_scale, bias_table, bias_index.reshape(1, pairs))
+    )(
+        in_hbm(note_feats), in_hbm(ehr_feats), in_hbm(note_head), in_hbm(ehr_head), logit_scale, in_hbm(bias_table),
+        in_hbm(bias_index.reshape(1, pairs)),
+    )
     loss, note_grad, ehr_grad = pl.pallas_call(
         write_out,
         out_shape=outs,
-        in_specs=[hbm] * 3,
+        in_specs=[whole] * 3,
         out_specs=(hbm,) * 3,
-        scratch_shapes=[vmem(out.shape, f32) for out in outs] + [dma((9,)), dma((9,))],
-        compiler_params=pltpu.CompilerParams(vmem_limit_bytes=62 * 1024 * 1024),
+        scratch_shapes=[dma((3,))],
+        compiler_params=pltpu.CompilerParams(vmem_limit_bytes=4 * 1024 * 1024),
     )(*results)
     return loss.reshape(pairs), note_grad, ehr_grad
 

time: 55.2 us -> 53.6 us (0.971)
  Pallas kernels: 53.5 us -> 52.2 us
    pallas_call x2, Pallas kernels: 53.5 us -> 52.2 us  [the longest x1 50.8 us: per_device(): pl.pallas_call(functools.partial(kernel, n_loop, ring), out_shape=tuple((...]
where the time goes in v3:
time: 53.6 us; the launch traced here: 53.5 us
  Pallas kernels  52.2 us (97%)
  between operations  1.29 us (2%)
    pallas_call x1, Pallas kernels, per_device(): pl.pallas_call(functools.partial(kernel, n_loop, ring), out_shape=tuple((...  50.8 us
    pallas_call x1, Pallas kernels, per_device(): pl.pallas_call(write_out, out_shape=outs, in_specs=[whole] * 3, out_specs...  1.35 us

profile of v3, /device:TPU:64, one launch (start us, length us, event | category | flops | bytes accessed | tf_op | source)
XLA Modules:
  0.0 53.5 jit_solution(17681494704672934405)
XLA Ops:
  1.3 50.8 %shard_map.94 = (f32[1,256]{1,0:T(1,128)S(1)}, f32[256,1024]{1,0:T(8,128)S(1)}, f32[256,1024]{1,0:T(8,128)S(1)}) custom-call(bf16[256,1024]{1,0:T(8,128)(2,1)} %nf_hbm.1, bf16[256,1024]{1,0:T(8,128)(2,1)} %ef_hbm.1, bf16[1024,1024]{1,0:T(8,128)(2,1)} %nh_hbm.1, bf16[1024,1024]{1,0:T(8,128)(2,1)} %eh_hbm.1, f32[1]{0:T(128)S(6)} %copy.10.scale_hbm, ...), custom_call_target="tpu_custom_call" | custom-call | tf_op jit(solution)/shard_map/pallas_call | solution.py:440
  52.1 1.3 %shard_map.95 = (f32[1,256]{1,0:T(1,128)}, f32[256,1024]{1,0:T(8,128)}, f32[256,1024]{1,0:T(8,128)}) custom-call(f32[1,256]{1,0:T(1,128)S(1)} %get-tuple-element.9.loss, f32[256,1024]{1,0:T(8,128)S(1)} %get-tuple-element.10.ng, f32[256,1024]{1,0:T(8,128)S(1)} %get-tuple-element.11.eg), custom_call_target="tpu_custom_call" | custom-call | tf_op jit(solution)/shard_map/pallas_call | solution.py:509

commit v4 on v3

--- a/solution.py
+++ b/solution.py
@@ -69,7 +69,8 @@
     l, o = lax.axis_index("loop"), lax.axis_index("outer")
     c, z, y = lax.rem(o, CORES), lax.rem(o // CORES, Z), o // (CORES * Z)
     x = lax.rem(l, X)
-    z_first = lax.rem((x + 1) // 2, 2) == 0
+    y_first = lax.rem((x + 1) // 2, 2)
+    z_first = y_first == 0
     side_a = x // 2
     side_b = 1 - side_a
     pod_a = lax.rem(l + n_loop - 1 + 2 * side_a, n_loop)
@@ -86,12 +87,23 @@
     sibling = (l, outer(y, z, 1 - c))
 
     barrier = pltpu.get_barrier_semaphore()
-    partners = [sibling]
-    partners += [(l, outer(yy, z, c)) for yy in ys[1:]] + [(l, outer(y, zz, c)) for zz in zs[1:]]
-    for pod in (below, above):
-        partners += [(pod, outer(yy, z, c)) for yy in ys] + [(pod, outer(y, zz, c)) for zz in zs[1:]]
-    for partner in partners:
-        pl.semaphore_signal(barrier, inc=1, device_id=partner, device_id_type=MESH)
+    partners = [(pod_a, outer(y, zz, c)) for zz in zs] + [(pod_b, outer(yy, z, c)) for yy in ys]
+    partners += [(l, outer(yy, z, c)) for yy in ys[1:]] + [(l, outer(y, zz, c)) for zz in zs[1:]] + [sibling]
+    also = {True: [(pod_b, outer(y, zz, c)) for zz in zs[1:]], False: [(pod_a, outer(yy, z, c)) for yy in ys[1:]]}
+
+    def greet(devices):
+        for device in devices:
+            pl.semaphore_signal(barrier, inc=1, device_id=device, device_id_type=MESH)
+
+    greet(partners)
+
+    @pl.when(z_first)
+    def _():
+        greet(also[True])
+
+    @pl.when(jnp.logical_not(z_first))
+    def _():
+        greet(also[False])
 
     top_rows, deep = pl.ds(0, 16), nh.shape[0] // HEAD_PARTS
     other_rows = pl.ds(16, pairs - 16)
@@ -141,7 +153,7 @@
     top = nu[0:8, :]
     top = top * lax.rsqrt(jnp.sum(top * top, axis=-1, keepdims=True) + 1e-06)
     own_piece[...] = pack(top).astype(jnp.bfloat16)
-    pl.semaphore_wait(barrier, len(partners))
+    pl.semaphore_wait(barrier, len(partners) + len(also[True]) + (len(also[False]) - len(also[True])) * y_first)
 
     def piece_sends(along_z):
         copies = []

time: 53.6 us -> 51.5 us (0.961)
  Pallas kernels: 52.2 us -> 50.1 us
    pallas_call x1, Pallas kernels: 50.8 us -> 48.7 us  [per_device(): pl.pallas_call(functools.partial(kernel, n_loop, ring), out_shape=tuple((...]
where the time goes in v4:
time: 51.5 us; the launch traced here: 51.3 us
  Pallas kernels  50.1 us (97%)
  between operations  1.29 us (3%)
    pallas_call x1, Pallas kernels, per_device(): pl.pallas_call(functools.partial(kernel, n_loop, ring), out_shape=tuple((...  48.7 us
    pallas_call x1, Pallas kernels, per_device(): pl.pallas_call(write_out, out_shape=outs, in_specs=[whole] * 3, out_specs...  1.35 us

profile of v4, /device:TPU:64, one launch (start us, length us, event | category | flops | bytes accessed | tf_op | source)
XLA Modules:
  0.0 51.3 jit_solution(10631566963297133425)
XLA Ops:
  1.3 48.7 %shard_map.94 = (f32[1,256]{1,0:T(1,128)S(1)}, f32[256,1024]{1,0:T(8,128)S(1)}, f32[256,1024]{1,0:T(8,128)S(1)}) custom-call(bf16[256,1024]{1,0:T(8,128)(2,1)} %nf_hbm.1, bf16[256,1024]{1,0:T(8,128)(2,1)} %ef_hbm.1, bf16[1024,1024]{1,0:T(8,128)(2,1)} %nh_hbm.1, bf16[1024,1024]{1,0:T(8,128)(2,1)} %eh_hbm.1, f32[1]{0:T(128)S(6)} %copy.10.scale_hbm, ...), custom_call_target="tpu_custom_call" | custom-call | tf_op jit(solution)/shard_map/pallas_call | solution.py:452
  50.0 1.3 %shard_map.95 = (f32[1,256]{1,0:T(1,128)}, f32[256,1024]{1,0:T(8,128)}, f32[256,1024]{1,0:T(8,128)}) custom-call(f32[1,256]{1,0:T(1,128)S(1)} %get-tuple-element.9.loss, f32[256,1024]{1,0:T(8,128)S(1)} %get-tuple-element.10.ng, f32[256,1024]{1,0:T(8,128)S(1)} %get-tuple-element.11.eg), custom_call_target="tpu_custom_call" | custom-call | tf_op jit(solution)/shard_map/pallas_call | solution.py:521

commit v5 on v4

--- a/solution.py
+++ b/solution.py
@@ -147,10 +147,13 @@
 
         lax.fori_loop(0, pairs // step_rows, step, 0)
 
-    for load in loads[: 2 + HEAD_PARTS]:
-        load.wait()
-    project(nf, nh, nu)
-    top = nu[0:8, :]
+    loads[0].wait()
+    top = None
+    for j in range(HEAD_PARTS):
+        loads[1 + j].wait()
+        part = dot(nf[0:16, j * deep : (j + 1) * deep], nh[j * deep : (j + 1) * deep, :])
+        top = part if top is None else top + part
+    top = top[0:8, :]
     top = top * lax.rsqrt(jnp.sum(top * top, axis=-1, keepdims=True) + 1e-06)
     own_piece[...] = pack(top).astype(jnp.bfloat16)
     pl.semaphore_wait(barrier, len(partners) + len(also[True]) + (len(also[False]) - len(also[True])) * y_first)
@@ -176,6 +179,8 @@
         for copy in piece_sends(False):
             copy.start()
 
+    loads[1 + HEAD_PARTS].wait()
+    project(nf, nh, nu)
     normalise(nu, ninv, ne)
 
     for load in loads[2 + HEAD_PARTS :]:

time: 51.5 us -> 51.5 us (level)
  no operation moved by 1% of the time
where the time goes in v5:
time: 51.5 us; the launch traced here: 51.3 us
  Pallas kernels  50.1 us (97%)
  between operations  1.29 us (3%)
    pallas_call x1, Pallas kernels, per_device(): pl.pallas_call(functools.partial(kernel, n_loop, ring), out_shape=tuple((...  48.7 us
    pallas_call x1, Pallas kernels, per_device(): pl.pallas_call(write_out, out_shape=outs, in_specs=[whole] * 3, out_specs...  1.35 us

profile of v5, /device:TPU:64, one launch (start us, length us, event | category | flops | bytes accessed | tf_op | source)
XLA Modules:
  0.0 51.3 jit_solution(16130297204949091563)
XLA Ops:
  1.3 48.7 %shard_map.94 = (f32[1,256]{1,0:T(1,128)S(1)}, f32[256,1024]{1,0:T(8,128)S(1)}, f32[256,1024]{1,0:T(8,128)S(1)}) custom-call(bf16[256,1024]{1,0:T(8,128)(2,1)} %nf_hbm.1, bf16[256,1024]{1,0:T(8,128)(2,1)} %ef_hbm.1, bf16[1024,1024]{1,0:T(8,128)(2,1)} %nh_hbm.1, bf16[1024,1024]{1,0:T(8,128)(2,1)} %eh_hbm.1, f32[1]{0:T(128)S(6)} %copy.10.scale_hbm, ...), custom_call_target="tpu_custom_call" | custom-call | tf_op jit(solution)/shard_map/pallas_call | solution.py:457
  50.0 1.3 %shard_map.95 = (f32[1,256]{1,0:T(1,128)}, f32[256,1024]{1,0:T(8,128)}, f32[256,1024]{1,0:T(8,128)}) custom-call(f32[1,256]{1,0:T(1,128)S(1)} %get-tuple-element.9.loss, f32[256,1024]{1,0:T(8,128)S(1)} %get-tuple-element.10.ng, f32[256,1024]{1,0:T(8,128)S(1)} %get-tuple-element.11.eg), custom_call_target="tpu_custom_call" | custom-call | tf_op jit(solution)/shard_map/pallas_call | solution.py:526
